TPU v7x, 128 devices: a whole 4x4x4 slice. The times are simulated.
128 devices in a mesh: gx: 8 (over z, x_lo), gy: 16 (over x_hi, y, core).
Axes of the slice: x: 4 (x_hi: 2, x_lo: 2; x = x_hi * 2 + x_lo), y: 4, z: 4, core: 2. Of those that a mesh axis runs over, the one named last changes fastest.
Arguments:
- features: bfloat16 [2048, 16, 1024], P(('gx', 'gy')), may hold values from -6 to 6
- brick_position: int32 [2048], P(('gx', 'gy')), may hold values from -1 to 1023, as said below
- brick_count: int32 [128], P(('gx', 'gy')), may hold values from 1 to 16, as said below
- brick_moved: int32 [128], P(('gx', 'gy')), may hold values from 0 to 6, as said below
- weight: bfloat16 [3, 3, 3, 32, 32], replicated, may hold values from -0.21875 to 0.21875
- cotangent: bfloat16 [2048, 16, 1024], P(('gx', 'gy')), may hold values from -6 to 6
Outputs:
- conv_out: bfloat16 [2048, 16, 1024], P(('gx', 'gy'))
- input_grad: bfloat16 [2048, 16, 1024], P(('gx', 'gy'))
- weight_grad: float32 [3, 3, 3, 32, 32], replicated
Inputs may be any that keep to these rules, and one draw needn't show every extreme that they name: `brick_count`: slots at and past a device's count are not live. In every draw some device holds 16 live bricks and some device holds 1. A device hands on its last brick_moved live slots; brick_moved[d] <= brick_count[d] and brick_count[d] - brick_moved[d] + brick_moved[p] <= 16 for partner p. In every draw some device hands on 6 bricks. `brick_position`: brick row * 32 + brick column inside the device's tile; distinct among a device's live slots; -1 in slots that are not live.
All inputs are finite; a program needn't handle non-finite values.
Results may differ from a plain program's by a relative error of at most 0.001.
Values may be sent and summed in bfloat16 or wider, within the bound.
A program may use at most 256 MiB of HBM per device.

v0:
```python
import math

import jax
import jax.numpy as jnp
from jax import lax
from jax.experimental import pallas as pl
from jax.experimental.pallas import tpu as pltpu
from jax.sharding import PartitionSpec as P

TILE_BRICK_ROWS = 32
TILE_BRICK_COLS = 32
MOVE = 6
SLOTS = 16
SIDE = 16
CELLS = SLOTS * SIDE
WIDTH = 1024
LANES = 128
CAND = 640
CENTRE = 384
ROW_KEY = 1024.0
DEAD = -float(1 << 23)
DEAD_TARGET = -float(1 << 22)
BF = jnp.bfloat16
F32 = jnp.float32
MESH = pl.DeviceIdType.MESH
N_GX = 8
N_GY = 16
VMEM_BYTES = 49152 * 1024
NEAR = 16
FAR = 8
CHUNK = 256 // NEAR
WEST, EAST, NORTH, SOUTH = (0, -1), (0, 1), (-1, 0), (1, 0)
NORTH_WEST, NORTH_EAST, SOUTH_WEST, SOUTH_EAST = (-1, -1), (-1, 1), (1, -1), (1, 1)
STEPS = (WEST, EAST, NORTH, SOUTH, NORTH_WEST, NORTH_EAST, SOUTH_WEST, SOUTH_EAST)


def twice(steps):
    return tuple((2 * row, 2 * col) for row, col in steps)


def dot(a, b):
    return jnp.dot(a, b, preferred_element_type=F32)


def kernel(
    pos_hbm,
    moved_ref,
    x_hbm,
    c_hbm,
    w_hbm,
    conv_ref,
    grad_ref,
    sum_ref,
    pos_ref,
    c_ref,
    w_ref,
    lent,
    borrowed,
    lent_y,
    borrowed_y,
    y_ref,
    strips,
    cand_c,
    cand_s,
    key_send,
    key_side,
    key_edge,
    key_corner,
    col_key,
    hot_s,
    hot_c,
    wide,
    guest_g,
    guest_x,
    outer,
    band_f,
    band_b,
    part,
    inbox1,
    mine,
    inbox2,
    total,
    in_sems,
    key_sems,
    halo_sems,
    lend_sems,
    send1,
    recv1,
    send2,
    recv2,
    send3,
    recv3,
    ready,
):
    gx = lax.axis_index("gx")
    gy = lax.axis_index("gy")

    def there(step):
        row, col = gx + step[0], gy + step[1]
        return (row >= 0) & (row < N_GX) & (col >= 0) & (col < N_GY)

    def place(step):
        return jnp.clip(gx + step[0], 0, N_GX - 1), jnp.clip(gy + step[1], 0, N_GY - 1)

    def back(step):
        return -step[0], -step[1]

    def how_many(steps):
        return sum(jnp.where(there(step), 1, 0) for step in steps)

    def signal(semaphore, peer):
        pl.semaphore_signal(semaphore, inc=1, device_id=peer, device_id_type=MESH)

    def signal_steps(semaphore, steps):
        for step in steps:

            @pl.when(there(step))
            def _(step=step):
                signal(semaphore, place(step))

    x_lo, z = lax.rem(gx, 2), lax.div(gx, 2)
    x_hi, y, core = lax.div(gy, 8), lax.rem(lax.div(gy, 2), 4), lax.rem(gy, 2)

    def flip(bit, do):
        return 1 - bit if do else bit

    def flip2(value, by):
        low, high = lax.rem(value, 2), lax.div(value, 2)
        return flip(low, by % 2) + 2 * flip(high, by // 2)

    def near(k):
        to = (flip(x_lo, k & 1), flip(x_hi, k >> 1 & 1), flip(core, k >> 2 & 1))
        low = flip(lax.rem(z, 2), k >> 3)
        rank = to[0] + 2 * to[1] + 4 * to[2] + 8 * low
        return (4 * lax.div(z, 2) + 2 * low + to[0], 8 * to[1] + 2 * y + to[2]), rank

    def far(k):
        return (2 * flip2(z, 2 * (k & 1)) + x_lo, 8 * x_hi + 2 * flip2(y, k >> 1) + core)

    my_near = x_lo + 2 * x_hi + 4 * core + 8 * lax.rem(z, 2)
    my_far = lax.div(z, 2) + 2 * y
    partner = near(2)[0]

    @pl.when(how_many(STEPS) < len(STEPS))
    def _():
        key_side[...] = jnp.full(key_side.shape, DEAD, F32)
        key_edge[...] = jnp.full(key_edge.shape, DEAD, F32)
        key_corner[...] = jnp.full(key_corner.shape, DEAD, F32)
        for field in range(2):
            cand_c[field, CELLS : CELLS + 32, :] = jnp.zeros((32, WIDTH), BF)
            for s in range(2):
                cand_s[field, s, CELLS : 2 * CELLS + 64, :] = jnp.zeros((CELLS + 64, LANES), BF)

    barrier = pltpu.get_barrier_semaphore()
    far_side = [near(k)[0] for k in (2, 3, 6, 7)]
    for peer in far_side:
        signal(barrier, peer)
    signal_steps(barrier, STEPS)

    fetches = [
        pltpu.make_async_copy(src, dst, in_sems.at[at])
        for at, (src, dst) in enumerate(
            (
                (c_hbm, c_ref),
                (x_hbm, cand_c.at[0, pl.ds(0, CELLS), :]),
                (w_hbm, w_ref),
                (pos_hbm, pos_ref),
            )
        )
    ]
    for at in (3, 0, 1, 2):
        fetches[at].start()

    fetches[3].wait()
    count = sum(jnp.where(pos_ref[i] >= 0, 1, 0) for i in range(SLOTS))
    moved = moved_ref[0]
    kept = count - moved

    sub = lax.broadcasted_iota(jnp.int32, (SIDE, LANES), 0)
    lane = lax.broadcasted_iota(jnp.int32, (8, CELLS), 1)
    lane_edge = lax.broadcasted_iota(jnp.int32, (8, LANES), 1)
    row_key = jnp.full((8, CELLS), DEAD, F32)
    north_key = jnp.full((8, LANES), DEAD, F32)
    for i in range(SLOTS):
        at = pos_ref[i]
        at = jnp.clip(at, 0, TILE_BRICK_ROWS * TILE_BRICK_COLS - 1)
        brick_row = gx * TILE_BRICK_ROWS + lax.shift_right_logical(at, 5)
        brick_col = gy * TILE_BRICK_COLS + lax.bitwise_and(at, 31)
        key = brick_row * (SIDE * 1024) + brick_col
        live = i < count
        target = jnp.where(live, key, int(DEAD_TARGET))
        source = jnp.where(live, key, int(DEAD))
        col_key[i * SIDE : (i + 1) * SIDE, :] = (sub * 1024 + target).astype(F32)
        wide_key = (jnp.zeros((8, CELLS), jnp.int32) + source).astype(F32)
        row_key = jnp.where(lax.shift_right_logical(lane, 4) == i, wide_key, row_key)
        north_key = jnp.where(
            lax.bitwise_and(lane_edge, 15) == i, wide_key[:, :LANES], north_key
        )
    row_key = row_key + lax.bitwise_and(lane, 15).astype(F32) * ROW_KEY
    south_key = north_key + (SIDE - 1) * ROW_KEY
    dead = jnp.full((8, LANES), DEAD, F32)

    def between(low, value):
        return jnp.where((lane_edge >= low) & (lane_edge < low + 16), value, dead)

    key_send[0] = row_key[:, :LANES]
    key_send[1] = row_key[:, LANES:]
    key_send[2] = between(0, south_key)
    key_send[3] = between(16, north_key)
    key_send[4] = between(32, south_key)
    key_send[5] = between(48, north_key)

    pick_row = lax.broadcasted_iota(jnp.int32, (32, CELLS), 0)
    pick_col = lax.broadcasted_iota(jnp.int32, (32, CELLS), 1)
    picked = lax.bitwise_and(pick_row, 15) * SIDE + lax.shift_right_logical(pick_row, 4) * 15
    pick = jnp.where(pick_col == picked, 1.0, 0.0).astype(BF)
    fetches[1].wait()
    strips[0] = dot(pick, cand_c[0, :CELLS, :]).astype(BF)


    pl.semaphore_wait(barrier, how_many(STEPS) + len(far_side))

    def remote(src, dst, sems, at, peer):
        return pltpu.make_async_remote_copy(
            src_ref=src,
            dst_ref=dst,
            send_sem=sems.at[0, at],
            recv_sem=sems.at[1, at],
            device_id=peer,
            device_id_type=MESH,
        )

    def halo(field, bricks):
        last = pl.ds(WIDTH - LANES, LANES)
        first = pl.ds(0, LANES)
        n_rows, s_rows = pl.ds(0, 16), pl.ds(16, 16)
        edge_n, edge_s = pl.ds(CELLS, 16), pl.ds(CELLS + 16, 16)
        corner_n, corner_s = pl.ds(2 * CELLS + 32, 16), pl.ds(2 * CELLS + 48, 16)
        side = pl.ds(CELLS, CELLS)
        own = bricks
        s = strips.at[field]
        c = cand_c.at[field]
        left, right = cand_s.at[field, 0], cand_s.at[field, 1]
        plan = [
            (own.at[:, first], right.at[side, :], WEST),
            (own.at[:, last], left.at[side, :], EAST),
            (s.at[n_rows, :], c.at[edge_s, :], NORTH),
            (s.at[s_rows, :], c.at[edge_n, :], SOUTH),
            (s.at[n_rows, first], right.at[corner_s, :], NORTH_WEST),
            (s.at[n_rows, last], left.at[corner_s, :], NORTH_EAST),
            (s.at[s_rows, first], right.at[corner_n, :], SOUTH_WEST),
            (s.at[s_rows, last], left.at[corner_n, :], SOUTH_EAST),
        ]
        return [
            (remote(src, dst, halo_sems.at[field], at, place(step)), step)
            for at, (src, dst, step) in enumerate(plan)
        ]

    def start_all(copies):
        for copy, step in copies:

            @pl.when(there(step))
            def _(copy=copy):
                copy.start()

    def wait_all(copies):
        for copy, step in copies:

            @pl.when(there(back(step)))
            def _(copy=copy):
                copy.wait_recv()

            @pl.when(there(step))
            def _(copy=copy):
                copy.wait_send()

    lend = remote(lent, borrowed, lend_sems.at[0], 0, partner)
    row = pl.ds(0, 1)
    key_plan = [
        (key_send.at[pl.ds(0, 2), row], key_side.at[1, :, row], WEST),
        (key_send.at[pl.ds(0, 2), row], key_side.at[0, :, row], EAST),
        (key_send.at[3, row], key_edge.at[1, row], NORTH),
        (key_send.at[2, row], key_edge.at[0, row], SOUTH),
        (key_send.at[5, row], key_corner.at[1, 1, row], NORTH_WEST),
        (key_send.at[5, row], key_corner.at[0, 1, row], NORTH_EAST),
        (key_send.at[4, row], key_corner.at[1, 0, row], SOUTH_WEST),
        (key_send.at[4, row], key_corner.at[0, 0, row], SOUTH_EAST),
    ]
    keys = [
        (remote(src, dst, key_sems, at, place(step)), step)
        for at, (src, dst, step) in enumerate(key_plan)
    ]
    start_all(keys)
    x_halo = halo(0, cand_c.at[0, pl.ds(0, CELLS)])
    start_all(x_halo)
    fetches[0].wait()
    for j in range(MOVE):
        lent[j] = c_ref[jnp.clip(kept + j, 0, SLOTS - 1)]
    lend.start()

    def side_hot(s, tiles):
        for a in range(3):
            target = col_key[...] + ((a - 1) * ROW_KEY + (2 * s - 1))
            for t, candidate in tiles:
                hot = jnp.where(target == candidate, 1.0, 0.0).astype(BF)
                hot_s[s, a * CELLS : (a + 1) * CELLS, t * LANES : (t + 1) * LANES] = hot

    def centre_hot(tiles):
        for at, a in enumerate((0, 2)):
            target = col_key[...] + (a - 1) * ROW_KEY
            for t, candidate in tiles:
                hot = jnp.where(target == candidate, 1.0, 0.0).astype(BF)
                hot_c[at * CELLS : (at + 1) * CELLS, t * LANES : (t + 1) * LANES] = hot

    own_tiles = [(0, key_send[0, :1]), (1, key_send[1, :1])]
    for s in range(2):
        side_hot(s, own_tiles)
    centre_hot(own_tiles)

    for field in range(2):
        cand_c[field, CELLS + 32 :, :] = jnp.zeros((CENTRE - CELLS - 32, WIDTH), BF)
        for s in range(2):
            cand_s[field, s, 2 * CELLS + 64 :, :] = jnp.zeros((CAND - 2 * CELLS - 64, LANES), BF)

    fetches[2].wait()
    def strip_of(a, frame_in):
        blocks = []
        for b in (2, 1, 0):
            for frame_out in (0, 1):
                blocks.append(w_ref[a, b, frame_in - frame_out + 1].astype(F32))
        z = jnp.zeros((32, 256), F32)
        return jnp.concatenate([z] + blocks + [z], axis=1)

    for a in range(3):
        for frame_in in range(2):
            strip = strip_of(a, frame_in)
            at = 32 * frame_in
            for q in range(1, 7):
                start = 448 - 64 * q
                band_f[a, 64 * q + at : 64 * q + at + 32, :] = strip[
                    :, start : start + 256
                ].astype(BF)
            for q in (0, 7):
                band_f[a, 64 * q + at : 64 * q + at + 32, :] = jnp.zeros((32, 256), BF)
            for j in range(4):
                start = 192 - 64 * j
                band_b[2 - a, 64 * j + at : 64 * j + at + 32, :] = strip[
                    :, start : start + 512
                ].astype(BF)

    wait_all(keys)
    signal_steps(ready.at[0], twice(STEPS))
    edge_key = jnp.maximum(key_edge[0, :1], key_edge[1, :1])
    for s in range(2):
        corner_key = jnp.maximum(key_corner[s, 0, :1], key_corner[s, 1, :1])
        tail_key = jnp.maximum(edge_key, corner_key)
        side_hot(s, [(2, key_side[s, 0, :1]), (3, key_side[s, 1, :1]), (4, tail_key)])
    centre_hot([(2, edge_key)])

    def widen(field):
        c = cand_c.at[field]
        for s, (start, to) in enumerate(((WIDTH - LANES, 0), (0, WIDTH + LANES))):
            cs = cand_s.at[field, s]
            cs[:CELLS, :] = c[:CELLS, start : start + LANES]
            cs[2 * CELLS : 2 * CELLS + 32, :] = c[CELLS : CELLS + 32, start : start + LANES]
            found = dot(hot_s[s], cs[...]).astype(BF)
            for a in range(3):
                wide[field, a, :, :, to : to + LANES] = found[a * CELLS : (a + 1) * CELLS].reshape(
                    SLOTS, SIDE, LANES
                )
        found = dot(hot_c[...], c[...]).astype(BF)
        shape = (SLOTS, SIDE, WIDTH)
        wide[field, 0, :, :, LANES : LANES + WIDTH] = found[:CELLS].reshape(shape)
        wide[field, 1, :, :, LANES : LANES + WIDTH] = c[:CELLS, :].reshape(shape)
        wide[field, 2, :, :, LANES : LANES + WIDTH] = found[CELLS:].reshape(shape)

    def window(field, a, group):
        return wide[field, a, :, :, 256 * group : 256 * group + 512].reshape(CELLS, 512)

    wait_all(x_halo)
    widen(0)

    for i in range(SLOTS):
        own = c_ref[i]
        cand_c[1, i * SIDE : (i + 1) * SIDE, :] = lax.select(i < kept, own, jnp.zeros_like(own))
    flipped = cand_c[1, :CELLS, :].T
    for a in range(3):
        value = jnp.zeros((256, 512), F32)
        for group in range(4):
            value = value + dot(flipped[256 * group : 256 * group + 256, :], window(0, a, group))
        outer[a] = value
    for j in range(MOVE):
        for a in range(3):
            guest_x[a, j * SIDE : (j + 1) * SIDE, :] = wide[0, a, jnp.clip(kept + j, 0, SLOTS - 1)]
    for a in range(3):
        guest_x[a, MOVE * SIDE :, :] = jnp.zeros((LANES - MOVE * SIDE, WIDTH + 2 * LANES), BF)
    guest_g[MOVE * SIDE :, :] = jnp.zeros((LANES - MOVE * SIDE, WIDTH), BF)

    pl.semaphore_wait(ready.at[0], how_many(twice(STEPS)))
    signal_steps(ready.at[1], twice(twice(STEPS)))

    lend.wait()
    for j in range(MOVE):
        guest = borrowed[j]
        guest_g[j * SIDE : (j + 1) * SIDE, :] = lax.select(j < moved, guest, jnp.zeros_like(guest))
    flipped = guest_g[...].T
    low = lax.broadcasted_iota(jnp.int32, (32, LANES), 1)
    keep = low < 64
    blocks = []
    for a in range(3):
        both_parts = outer[a]
        for group in range(4):
            both_parts = both_parts + dot(
                flipped[256 * group : 256 * group + 256, :],
                guest_x[a, :, 256 * group : 256 * group + 512],
            )
        for b in range(3):
            sums = [jnp.zeros((64, LANES), F32), jnp.zeros((64, LANES), F32)]
            for j in range(4):
                column = j + b + 1
                tile = column // 2
                sums[column % 2] = (
                    sums[column % 2]
                    + both_parts[64 * j : 64 * j + 64, LANES * tile : LANES * tile + LANES]
                )
            both = sums[0] + pltpu.roll(sums[1], 64, 1)
            top = jnp.where(keep, both[:32], 0.0)
            bottom = jnp.where(keep, both[32:], 0.0)
            blocks.append(bottom + pltpu.roll(top, 32, 1))
    ninth = blocks[8]
    for s in range(3):
        piece = jnp.where((low >= 32 * s) & (low < 32 * s + 32), ninth, 0.0)
        blocks[s] = blocks[s] + pltpu.roll(piece, 96 - 32 * s, 1)
    for ab in range(8):
        part[32 * ab : 32 * ab + 32, :] = blocks[ab]

    round1 = []
    for k in range(1, NEAR):
        peer, rank = near(k)
        round1.append(
            pltpu.make_async_remote_copy(
                src_ref=part.at[pl.ds(pl.multiple_of(rank * CHUNK, CHUNK), CHUNK), :],
                dst_ref=inbox1.at[k],
                send_sem=send1.at[k],
                recv_sem=recv1.at[k],
                device_id=peer,
                device_id_type=MESH,
            )
        )
    for copy in round1:
        copy.start()

    for i in range(SLOTS):
        guest = borrowed[jnp.clip(i - kept, 0, MOVE - 1)]
        value = lax.select(
            i < kept, c_ref[i], lax.select(i < count, guest, jnp.zeros_like(guest))
        )
        cand_c[1, i * SIDE : (i + 1) * SIDE, :] = value
    strips[1] = dot(pick, cand_c[1, :CELLS, :]).astype(BF)
    g_halo = halo(1, cand_c.at[1, pl.ds(0, CELLS)])
    start_all(g_halo)

    def convolve(field, apply):
        for group in range(4):
            value = jnp.zeros((CELLS, 256), F32)
            for a in range(3):
                value = value + apply(a, window(field, a, group))
            yield group, value

    slot_row = lax.broadcasted_iota(jnp.int32, (CELLS, 256), 0)
    live_rows = slot_row < count * SIDE
    for group, value in convolve(0, lambda a, rows: dot(rows, band_f[a])):
        value = jnp.where(live_rows, value, 0.0).astype(BF)
        y_ref[:, :, 256 * group : 256 * group + 256] = value.reshape(SLOTS, SIDE, 256)
    for j in range(MOVE):
        brick = y_ref[jnp.clip(kept + j, 0, SLOTS - 1)]
        lent_y[j] = lax.select(j < moved, brick, jnp.zeros_like(brick))
    lend_y = remote(lent_y, borrowed_y, lend_sems.at[1], 0, partner)

    for copy in round1:
        copy.wait_recv()
    own_chunk = pl.ds(pl.multiple_of(my_near * CHUNK, CHUNK), CHUNK)
    own_rows = part[own_chunk, :]
    for k in range(1, NEAR):
        own_rows = own_rows + inbox1[k]
    mine[...] = own_rows
    inbox2[my_far] = own_rows
    pl.semaphore_wait(ready.at[1], how_many(twice(twice(STEPS))))
    round2 = []
    for k in range(1, FAR):
        round2.append(
            pltpu.make_async_remote_copy(
                src_ref=mine,
                dst_ref=inbox2.at[my_far],
                send_sem=send2.at[k],
                recv_sem=recv2.at[k],
                device_id=far(k),
                device_id_type=MESH,
            )
        )
    for copy in round2:
        copy.start()

    lend_y.start()

    wait_all(g_halo)
    widen(1)
    by_rows = (((1,), (1,)), ((), ()))
    for group, value in convolve(
        1,
        lambda a, rows: lax.dot_general(rows, band_b[a], by_rows, preferred_element_type=F32),
    ):
        value = jnp.where(live_rows, value, 0.0).astype(BF)
        grad_ref[:, :, 256 * group : 256 * group + 256] = value.reshape(SLOTS, SIDE, 256)

    for copy in round2:
        copy.wait_recv()
    chunk_sum = inbox2[0]
    for k in range(1, FAR):
        chunk_sum = chunk_sum + inbox2[k]
    total[own_chunk, :] = chunk_sum * (1.0 / math.sqrt(N_GX * N_GY * SLOTS * SIDE * SIDE * 2))
    round3 = []
    for k in range(1, NEAR):
        round3.append(
            pltpu.make_async_remote_copy(
                src_ref=total.at[own_chunk, :],
                dst_ref=total.at[own_chunk, :],
                send_sem=send3.at[k],
                recv_sem=recv3.at[k],
                device_id=near(k)[0],
                device_id_type=MESH,
            )
        )
    for copy in round3:
        copy.start()

    lend_y.wait()
    for i in range(SLOTS):
        guest = borrowed_y[jnp.clip(i - kept, 0, MOVE - 1)]
        guest = lax.select(i < kept + MOVE, guest, jnp.zeros_like(guest))
        conv_ref[i] = lax.select(i < kept, y_ref[i], guest)

    for copy in round1:
        copy.wait_send()
    for copy in round2:
        copy.wait_send()
    for copy in round3:
        copy.wait()
    sum_ref[...] = total[...]


def finish(conv_ref, grad_ref, sum_ref, conv_hbm, grad_hbm, wg_hbm, wg_ref, sems):
    conv_copy = pltpu.make_async_copy(conv_ref, conv_hbm, sems.at[0])
    grad_copy = pltpu.make_async_copy(grad_ref, grad_hbm, sems.at[1])
    conv_copy.start()
    grad_copy.start()
    for h in range(2):
        turned = sum_ref[128 * h : 128 * h + 128, :].T
        for at in range(4):
            ab = 4 * h + at
            for s in range(3):
                wg_ref[ab // 3, ab % 3, s] = turned[32 * s : 32 * s + 32, 32 * at : 32 * at + 32]
        if h == 0:
            for s in range(3):
                wg_ref[2, 2, s] = turned[96:128, 32 * s : 32 * s + 32]
    wg_copy = pltpu.make_async_copy(wg_ref, wg_hbm, sems.at[2])
    wg_copy.start()
    conv_copy.wait()
    grad_copy.wait()
    wg_copy.wait()


def local(features, brick_position, brick_count, brick_moved, weight, cotangent):
    smem = pl.BlockSpec(memory_space=pltpu.SMEM)
    vmem = pl.BlockSpec(memory_space=pltpu.VMEM)
    hbm = pl.BlockSpec(memory_space=pltpu.HBM)
    bricks = (SLOTS, SIDE, WIDTH)
    taps = (3, 3, 3, 32, 32)
    dma = pltpu.SemaphoreType.DMA
    conv, grad, summed = pl.pallas_call(
        kernel,
        out_shape=(
            pltpu.VMEM(bricks, BF),
            pltpu.VMEM(bricks, BF),
            pltpu.VMEM((256, LANES), F32),
        ),
        in_specs=[hbm, smem, hbm, hbm, hbm],
        out_specs=(vmem, vmem, vmem),
        scratch_shapes=[
            pltpu.SMEM((SLOTS,), jnp.int32),
            pltpu.VMEM(bricks, BF),
            pltpu.VMEM(taps, BF),
            pltpu.VMEM((MOVE, SIDE, WIDTH), BF),
            pltpu.VMEM((MOVE, SIDE, WIDTH), BF),
            pltpu.VMEM((MOVE, SIDE, WIDTH), BF),
            pltpu.VMEM((MOVE, SIDE, WIDTH), BF),
            pltpu.VMEM(bricks, BF),
            pltpu.VMEM((2, 32, WIDTH), BF),
            pltpu.VMEM((2, CENTRE, WIDTH), BF),
            pltpu.VMEM((2, 2, CAND, LANES), BF),
            pltpu.VMEM((6, 8, LANES), F32),
            pltpu.VMEM((2, 2, 8, LANES), F32),
            pltpu.VMEM((2, 8, LANES), F32),
            pltpu.VMEM((2, 2, 8, LANES), F32),
            pltpu.VMEM((CELLS, LANES), F32),
            pltpu.VMEM((2, 3 * CELLS, CAND), BF),
            pltpu.VMEM((2 * CELLS, CENTRE), BF),
            pltpu.VMEM((2, 3, SLOTS, SIDE, WIDTH + 2 * LANES), BF),
            pltpu.VMEM((LANES, WIDTH), BF),
            pltpu.VMEM((3, LANES, WIDTH + 2 * LANES), BF),
            pltpu.VMEM((3, 256, 512), F32),
            pltpu.VMEM((3, 512, 256), BF),
            pltpu.VMEM((3, 256, 512), BF),
            pltpu.VMEM((256, LANES), F32),
            pltpu.VMEM((NEAR, CHUNK, LANES), F32),
            pltpu.VMEM((CHUNK, LANES), F32),
            pltpu.VMEM((FAR, CHUNK, LANES), F32),
            pltpu.VMEM((256, LANES), F32),
            dma((4,)),
            dma((2, 8)),
            dma((2, 2, 8)),
            dma((2, 2, 1)),
            dma((NEAR,)),
            dma((NEAR,)),
            dma((FAR,)),
            dma((FAR,)),
            dma((NEAR,)),
            dma((NEAR,)),
            pltpu.SemaphoreType.REGULAR((2,)),
        ],
        compiler_params=pltpu.CompilerParams(
            collective_id=0, has_side_effects=True, vmem_limit_bytes=VMEM_BYTES
        ),
    )(
        pltpu.with_memory_space_constraint(brick_position, pltpu.HBM),
        brick_moved,
        pltpu.with_memory_space_constraint(features.reshape(CELLS, WIDTH), pltpu.HBM),
        pltpu.with_memory_space_constraint(cotangent, pltpu.HBM),
        pltpu.with_memory_space_constraint(weight, pltpu.HBM),
    )
    return pl.pallas_call(
        finish,
        out_shape=(
            jax.ShapeDtypeStruct(bricks, BF),
            jax.ShapeDtypeStruct(bricks, BF),
            jax.ShapeDtypeStruct(taps, F32),
        ),
        in_specs=[vmem, vmem, vmem],
        out_specs=(hbm, hbm, hbm),
        scratch_shapes=[
            pltpu.VMEM(taps, F32),
            dma((3,)),
        ],
        compiler_params=pltpu.CompilerParams(vmem_limit_bytes=8 * 1024 * 1024),
    )(conv, grad, summed)


def solution(mesh):
    placed = (
        P(("gx", "gy"), None, None),
        P(("gx", "gy")),
        P(("gx", "gy")),
        P(("gx", "gy")),
        P(),
        P(("gx", "gy"), None, None),
    )
    return jax.shard_map(
        local,
        mesh=mesh,
        in_specs=placed,
        out_specs=(P(("gx", "gy"), None, None), P(("gx", "gy"), None, None), P()),
        check_vma=False,
    )
```

profile of v0, /device:TPU:1, one launch (start us, length us, event | category | flops | bytes accessed | tf_op | source)
XLA Modules:
  0.0 35.5 jit_solution(6161985934943195987)
XLA Ops:
  1.3 33.0 %shard_map.76 = (bf16[16,16,1024]{2,1,0:T(8,128)(2,1)S(1)}, bf16[16,16,1024]{2,1,0:T(8,128)(2,1)S(1)}, f32[256,128]{1,0:T(8,128)S(1)}) custom-call(s32[16]{0:T(128)} %pos_hbm.1, s32[1]{0:T(128)S(6)} %copy.8.moved_ref, bf16[256,1024]{1,0:T(8,128)(2,1)} %bitcast.1, bf16[16,16,1024]{2,1,0:T(8,128)(2,1)} %c_hbm.1, bf16[3,3,3,32,32]{4,3,2,1,0:T(8,128)(2,1)} %w_hbm.1), custom_call_target="tpu_custom_call" | custom-call | tf_op jit(solution)/shard_map/pallas_call | solution.py:580
  34.3 1.1 %shard_map.77 = (bf16[16,16,1024]{2,1,0:T(8,128)(2,1)}, bf16[16,16,1024]{2,1,0:T(8,128)(2,1)}, f32[3,3,3,32,32]{4,3,2,1,0:T(8,128)}) custom-call(bf16[16,16,1024]{2,1,0:T(8,128)(2,1)S(1)} %get-tuple-element.6.conv_ref, bf16[16,16,1024]{2,1,0:T(8,128)(2,1)S(1)} %get-tuple-element.7.grad_ref, f32[256,128]{1,0:T(8,128)S(1)} %get-tuple-element.8.sum_ref), custom_call_target="tpu_custom_call" | custom-call | tf_op jit(solution)/shard_map/pallas_call | solution.py:641
where the time goes:
time: 35.6 us; the launch traced here: 35.5 us
  Pallas kernels  34.2 us (96%)
  between operations  1.28 us (4%)
    pallas_call x1, Pallas kernels, local(): pl.pallas_call(kernel, out_shape=(pltpu.VMEM(bricks, BF), pltpu.VMEM(bric...  33 us
    pallas_call x1, Pallas kernels, local(): pl.pallas_call(finish, out_shape=(jax.ShapeDtypeStruct(bricks, BF), jax.S...  1.14 us

commit v1 on v0

--- a/solution.py
+++ b/solution.py
@@ -31,7 +31,9 @@
 CHUNK = 256 // NEAR
 WEST, EAST, NORTH, SOUTH = (0, -1), (0, 1), (-1, 0), (1, 0)
 NORTH_WEST, NORTH_EAST, SOUTH_WEST, SOUTH_EAST = (-1, -1), (-1, 1), (1, -1), (1, 1)
-STEPS = (WEST, EAST, NORTH, SOUTH, NORTH_WEST, NORTH_EAST, SOUTH_WEST, SOUTH_EAST)
+STEPS = (NORTH_WEST, NORTH_EAST, SOUTH_WEST, SOUTH_EAST, NORTH, SOUTH, WEST, EAST)
+NEAR_ORDER = (10, 14, 11, 15, 2, 6, 3, 7, 9, 13, 8, 12, 1, 5, 4)
+FAR_ORDER = (5, 7, 4, 6, 3, 1, 2)
 
 
 def twice(steps):
@@ -270,6 +272,9 @@
             def _(copy=copy):
                 copy.wait_recv()
 
+    def wait_sent(copies):
+        for copy, step in copies:
+
             @pl.when(there(step))
             def _(copy=copy):
                 copy.wait_send()
@@ -435,7 +440,7 @@
         part[32 * ab : 32 * ab + 32, :] = blocks[ab]
 
     round1 = []
-    for k in range(1, NEAR):
+    for k in NEAR_ORDER:
         peer, rank = near(k)
         round1.append(
             pltpu.make_async_remote_copy(
@@ -487,7 +492,7 @@
     inbox2[my_far] = own_rows
     pl.semaphore_wait(ready.at[1], how_many(twice(twice(STEPS))))
     round2 = []
-    for k in range(1, FAR):
+    for k in FAR_ORDER:
         round2.append(
             pltpu.make_async_remote_copy(
                 src_ref=mine,
@@ -520,7 +525,7 @@
         chunk_sum = chunk_sum + inbox2[k]
     total[own_chunk, :] = chunk_sum * (1.0 / math.sqrt(N_GX * N_GY * SLOTS * SIDE * SIDE * 2))
     round3 = []
-    for k in range(1, NEAR):
+    for k in NEAR_ORDER:
         round3.append(
             pltpu.make_async_remote_copy(
                 src_ref=total.at[own_chunk, :],
@@ -540,6 +545,8 @@
         guest = lax.select(i < kept + MOVE, guest, jnp.zeros_like(guest))
         conv_ref[i] = lax.select(i < kept, y_ref[i], guest)
 
+    for copies in (keys, x_halo, g_halo):
+        wait_sent(copies)
     for copy in round1:
         copy.wait_send()
     for copy in round2:

time: 35.6 us -> 34.5 us (0.969)
  Pallas kernels: 34.2 us -> 33.1 us
    pallas_call x1, Pallas kernels: 33 us -> 32 us  [local(): pl.pallas_call(kernel, out_shape=(pltpu.VMEM(bricks, BF), pltpu.VMEM(bric...]
where the time goes in v1:
time: 34.5 us; the launch traced here: 34.4 us
  Pallas kernels  33.1 us (96%)
  between operations  1.28 us (4%)
    pallas_call x1, Pallas kernels, local(): pl.pallas_call(kernel, out_shape=(pltpu.VMEM(bricks, BF), pltpu.VMEM(bric...  32 us
    pallas_call x1, Pallas kernels, local(): pl.pallas_call(finish, out_shape=(jax.ShapeDtypeStruct(bricks, BF), jax.S...  1.14 us

profile of v1, /device:TPU:1, one launch (start us, length us, event | category | flops | bytes accessed | tf_op | source)
XLA Modules:
  0.0 34.4 jit_solution(9588277446890583114)
XLA Ops:
  1.3 32.0 %shard_map.76 = (bf16[16,16,1024]{2,1,0:T(8,128)(2,1)S(1)}, bf16[16,16,1024]{2,1,0:T(8,128)(2,1)S(1)}, f32[256,128]{1,0:T(8,128)S(1)}) custom-call(s32[16]{0:T(128)} %pos_hbm.1, s32[1]{0:T(128)S(6)} %copy.8.moved_ref, bf16[256,1024]{1,0:T(8,128)(2,1)} %bitcast.1, bf16[16,16,1024]{2,1,0:T(8,128)(2,1)} %c_hbm.1, bf16[3,3,3,32,32]{4,3,2,1,0:T(8,128)(2,1)} %w_hbm.1), custom_call_target="tpu_custom_call" | custom-call | tf_op jit(solution)/shard_map/pallas_call | solution.py:587
  33.3 1.1 %shard_map.77 = (bf16[16,16,1024]{2,1,0:T(8,128)(2,1)}, bf16[16,16,1024]{2,1,0:T(8,128)(2,1)}, f32[3,3,3,32,32]{4,3,2,1,0:T(8,128)}) custom-call(bf16[16,16,1024]{2,1,0:T(8,128)(2,1)S(1)} %get-tuple-element.6.conv_ref, bf16[16,16,1024]{2,1,0:T(8,128)(2,1)S(1)} %get-tuple-element.7.grad_ref, f32[256,128]{1,0:T(8,128)S(1)} %get-tuple-element.8.sum_ref), custom_call_target="tpu_custom_call" | custom-call | tf_op jit(solution)/shard_map/pallas_call | solution.py:648

commit v2 on v1

--- a/solution.py
+++ b/solution.py
@@ -296,11 +296,11 @@
         for at, (src, dst, step) in enumerate(key_plan)
     ]
     start_all(keys)
-    x_halo = halo(0, cand_c.at[0, pl.ds(0, CELLS)])
-    start_all(x_halo)
     fetches[0].wait()
     for j in range(MOVE):
         lent[j] = c_ref[jnp.clip(kept + j, 0, SLOTS - 1)]
+    x_halo = halo(0, cand_c.at[0, pl.ds(0, CELLS)])
+    start_all(x_halo)
     lend.start()
 
     def side_hot(s, tiles):

time: 34.5 us -> 34.6 us (level)
  no operation moved by 1% of the time
where the time goes in v2:
time: 34.6 us; the launch traced here: 34.4 us
  Pallas kernels  33.1 us (96%)
  between operations  1.28 us (4%)
    pallas_call x1, Pallas kernels, local(): pl.pallas_call(kernel, out_shape=(pltpu.VMEM(bricks, BF), pltpu.VMEM(bric...  32 us
    pallas_call x1, Pallas kernels, local(): pl.pallas_call(finish, out_shape=(jax.ShapeDtypeStruct(bricks, BF), jax.S...  1.14 us

profile of v2, /device:TPU:1, one launch (start us, length us, event | category | flops | bytes accessed | tf_op | source)
XLA Modules:
  0.0 34.4 jit_solution(7435779492772505099)
XLA Ops:
  1.3 32.0 %shard_map.76 = (bf16[16,16,1024]{2,1,0:T(8,128)(2,1)S(1)}, bf16[16,16,1024]{2,1,0:T(8,128)(2,1)S(1)}, f32[256,128]{1,0:T(8,128)S(1)}) custom-call(s32[16]{0:T(128)} %pos_hbm.1, s32[1]{0:T(128)S(6)} %copy.8.moved_ref, bf16[256,1024]{1,0:T(8,128)(2,1)} %bitcast.1, bf16[16,16,1024]{2,1,0:T(8,128)(2,1)} %c_hbm.1, bf16[3,3,3,32,32]{4,3,2,1,0:T(8,128)(2,1)} %w_hbm.1), custom_call_target="tpu_custom_call" | custom-call | tf_op jit(solution)/shard_map/pallas_call | solution.py:587
  33.3 1.1 %shard_map.77 = (bf16[16,16,1024]{2,1,0:T(8,128)(2,1)}, bf16[16,16,1024]{2,1,0:T(8,128)(2,1)}, f32[3,3,3,32,32]{4,3,2,1,0:T(8,128)}) custom-call(bf16[16,16,1024]{2,1,0:T(8,128)(2,1)S(1)} %get-tuple-element.6.conv_ref, bf16[16,16,1024]{2,1,0:T(8,128)(2,1)S(1)} %get-tuple-element.7.grad_ref, f32[256,128]{1,0:T(8,128)S(1)} %get-tuple-element.8.sum_ref), custom_call_target="tpu_custom_call" | custom-call | tf_op jit(solution)/shard_map/pallas_call | solution.py:648
